TPU v7x, 128 devices: a whole 4x4x4 slice. The times are simulated.
128 devices in a mesh: mesh: 8 (over x, core), chan: 16 (over z, y).
Axes of the slice: x: 4, y: 4, z: 4, core: 2. Of those that a mesh axis runs over, the one named last changes fastest.
Arguments:
- node_latents: bfloat16 [16384, 512], P(('mesh', 'chan')), may hold values from -6 to 6
- edge_latents: bfloat16 [131072, 512], P(('mesh', 'chan')), may hold values from -6 to 6
- sender_slot: int32 [131072], P(('mesh', 'chan')), may hold values from 0 to 2175, as said below
- receiver_node: int32 [131072], P(('mesh', 'chan')), may hold values from 0 to 127, as said below
- send_rows: int32 [16384, 16], P(('mesh', 'chan')), may hold values from 0 to 127
- edge_in: bfloat16 [2, 3, 512, 512], P(None, None, 'chan'), may hold values from -0.15625 to 0.15625
- edge_out: bfloat16 [2, 512, 512], P(None, 'chan'), may hold values from -0.25 to 0.25
- node_in: bfloat16 [2, 2, 512, 512], P(None, None, 'chan'), may hold values from -0.1875 to 0.1875
- node_out: bfloat16 [2, 512, 512], P(None, 'chan'), may hold values from -0.25 to 0.25
Outputs:
- node_state: bfloat16 [16384, 512], P(('mesh', 'chan'))
- edge_state: bfloat16 [131072, 512], P(('mesh', 'chan'))
Inputs may be any that keep to these rules, and one draw needn't show every extreme that they name: `sender_slot`: below 128 a node of the edge's own device; 128 + p * 16 + s names slot s of what device p sends to the edge's device, p never the device itself; both ends of the range occur in every draw. `receiver_node`: sorted within each device's 1024 edges.
All inputs are finite; a program needn't handle non-finite values.
Results may differ from a plain program's by a relative error of at most 0.014.
Values may be sent and summed in bfloat16 or wider, within the bound.
A program may use at most 64 MiB of HBM per device.

v0:
```python
import jax
import jax.numpy as jnp
from jax import lax
from jax.sharding import PartitionSpec as P


def norm_rows(output, width):
    row_mean = jnp.sum(output, axis=1, keepdims=True) / width
    row_square = jnp.sum(output * output, axis=1, keepdims=True) / width
    return (output - row_mean) * lax.rsqrt(row_square - row_mean * row_mean + 1e-05)


def make_adder(left, total, piece):
    return total + jnp.dot(left, piece, preferred_element_type=jnp.float32)


def make_pair_adder(first, second, total, piece):
    total = jnp.dot(first, piece[0], preferred_element_type=jnp.float32)
    return total + jnp.dot(second, piece[1], preferred_element_type=jnp.float32)


def make_projector(left, piece):
    first_sum = jnp.dot(left, piece[0], preferred_element_type=jnp.float32)
    second_sum = jnp.dot(left, piece[1], preferred_element_type=jnp.float32)
    return (first_sum, second_sum)


def local(
    node_latents,
    edge_latents,
    sender_slot,
    receiver_node,
    send_rows,
    edge_in,
    edge_out,
    node_in,
    node_out,
):
    round_count = edge_in.shape[0]
    node_count = node_latents.shape[0]
    width = node_latents.shape[1]
    edge_count = edge_latents.shape[0]
    peer_count = send_rows.shape[0]
    slot_count = send_rows.shape[1]
    flat_rows = send_rows.reshape(peer_count * slot_count)
    node_state = node_latents
    edge_state = edge_latents
    for round_index in range(round_count):
        empty_nodes = jnp.zeros((node_count, width), jnp.float32)
        empty_edges = jnp.zeros((edge_count, width), jnp.float32)
        send_full, recv_full = make_projector(
            node_state, lax.all_gather(edge_in[round_index, 1:3], "chan", axis=1, tiled=True)
        )
        send_proj = send_full.astype(jnp.bfloat16)
        recv_proj = recv_full.astype(jnp.bfloat16)
        outgoing = send_proj[flat_rows]
        incoming = lax.all_to_all(
            outgoing, ("mesh", "chan"), split_axis=0, concat_axis=0, tiled=True
        )
        send_table = jnp.concatenate([send_proj, incoming], axis=0)
        endpoint_sum = send_table[sender_slot].astype(jnp.float32) + recv_proj[
            receiver_node
        ].astype(jnp.float32)
        preact = make_adder(
            edge_state,
            endpoint_sum,
            lax.all_gather(edge_in[round_index, 0], "chan", axis=0, tiled=True),
        )
        edge_hidden = jax.nn.silu(preact).astype(jnp.bfloat16)
        output = make_adder(
            edge_hidden,
            empty_edges,
            lax.all_gather(edge_out[round_index], "chan", axis=0, tiled=True),
        )
        edge_state = (edge_state.astype(jnp.float32) + norm_rows(output, width)).astype(
            jnp.bfloat16
        )
        aggregate = jax.ops.segment_sum(
            edge_state.astype(jnp.float32),
            receiver_node,
            num_segments=node_count,
            indices_are_sorted=True,
        ).astype(jnp.bfloat16)
        preact = make_pair_adder(
            node_state,
            aggregate,
            empty_nodes,
            lax.all_gather(node_in[round_index], "chan", axis=1, tiled=True),
        )
        node_hidden = jax.nn.silu(preact).astype(jnp.bfloat16)
        output = make_adder(
            node_hidden,
            empty_nodes,
            lax.all_gather(node_out[round_index], "chan", axis=0, tiled=True),
        )
        node_state = (node_state.astype(jnp.float32) + norm_rows(output, width)).astype(
            jnp.bfloat16
        )
    return (node_state, edge_state)


def solution(mesh):
    in_specs = (
        P(("mesh", "chan"), None),
        P(("mesh", "chan"), None),
        P(("mesh", "chan")),
        P(("mesh", "chan")),
        P(("mesh", "chan"), None),
        P(None, None, "chan", None),
        P(None, "chan", None),
        P(None, None, "chan", None),
        P(None, "chan", None),
    )
    out_specs = (P(("mesh", "chan"), None), P(("mesh", "chan"), None))
    return jax.shard_map(local, mesh=mesh, in_specs=in_specs, out_specs=out_specs, check_vma=False)
```

profile of v0, /device:TPU:0, one launch (start us, length us, event | category | flops | bytes accessed | tf_op | source)
XLA Modules:
  0.0 356.2 jit_solution(1383066154428400178)
XLA Ops:
  7.2 1.5 fusion.37
  8.8 1.5 fusion.38
  10.4 0.7 all-gather.21.cloned.1.call-update
  11.1 0.8 copy.14
  11.9 0.1 reshape.111
  12.0 44.1 %all-gather.17.cloned.1.call-done = bf16[1,2,512,512]{3,2,1,0:T(8,128)(2,1)} async-done(((bf16[1,2,32,512]{3,2,1,0:T(8,128)(2,1)}), bf16[1,2,512,512]{3,2,1,0:T(8,128)(2,1)}) %all-gather.17.cloned.1.call-update) | async-done | bytes 1048592 | tf_op jit(solution)/shard_map/all_gather | solution.py:52
  56.1 1.3 convolution_convert_fusion.3
  57.4 9.2 %gather_fusion = bf16[2048,512]{1,0:T(8,128)(2,1)} fusion(bf16[128,512]{1,0:T(8,128)(2,1)S(1)} %convolution_convert_fusion.3, s32[2048]{0:T(1024)S(1)} %broadcast_clamp_fusion), kind=kCustom, calls=%fused_computation | custom fusion | bytes 4202496 | tf_op jit(solution)/shard_map/gather | solution.py:56
  66.6 7.9 %all-to-all-start = ((bf16[128,16,512]{2,1,0:T(8,128)(2,1)}), bf16[128,16,512]{2,1,0:T(8,128)(2,1)S(1)}, u32[]{:S(2)}, u32[]{:S(2)}) async-start(bf16[128,16,512]{2,1,0:T(8,128)(2,1)} %bitcast.3), calls=%async_computation | async-start | bytes 4194304 | tf_op jit(solution)/shard_map/all_to_all | solution.py:57
  74.6 0.5 all-gather.19.cloned.1.call-update
  75.2 1.5 copy.13
  76.7 1.4 fusion.36
  78.1 39.6 %all-gather.2 = bf16[1,1,512,512]{3,2,1,0:T(8,128)(2,1)} all-gather(bf16[1,1,32,512]{3,2,1,0:T(8,128)(2,1)S(1)} %get-tuple-element.15), channel_id=4, replica_groups=mesh['mesh'=8,'chan'=16] {'chan'}, dimensions={2}, use_global_device_ids=true | all-gather | bytes 557056 | tf_op jit(solution)/shard_map/all_gather | solution.py:67
  117.7 0.6 fusion.39
  118.3 24.4 %all-gather.3 = bf16[1,512,512]{2,1,0:T(8,128)(2,1)} all-gather(bf16[1,32,512]{2,1,0:T(8,128)(2,1)S(1)} %get-tuple-element.21), channel_id=5, replica_groups=mesh['mesh'=8,'chan'=16] {'chan'}, dimensions={1}, use_global_device_ids=true | all-gather | bytes 557056 | tf_op jit(solution)/shard_map/all_gather | solution.py:73
  142.7 1.4 fusion.40
  144.1 25.0 %all-gather.4 = bf16[1,512,512]{2,1,0:T(8,128)(2,1)} all-gather(bf16[1,32,512]{2,1,0:T(8,128)(2,1)S(1)} %get-tuple-element.22), channel_id=6, replica_groups=mesh['mesh'=8,'chan'=16] {'chan'}, dimensions={1}, use_global_device_ids=true | all-gather | bytes 557056 | tf_op jit(solution)/shard_map/all_gather | solution.py:94
  169.2 1.3 convolution_convert_fusion.2
  170.4 5.1 %gather_fusion.2 = bf16[1024,512]{1,0:T(8,128)(2,1)} fusion(bf16[128,512]{1,0:T(8,128)(2,1)S(1)} %convolution_convert_fusion.2, s32[1024]{0:T(1024)S(1)} %fusion.27), kind=kCustom, calls=%fused_computation.2 | custom fusion | bytes 2101248 | tf_op jit(solution)/shard_map/gather | solution.py:61
  175.5 2.0 fusion.5
  177.5 1.3 copy-done
  178.8 1.8 pad_maximum_fusion
  180.6 5.1 %gather_fusion.1 = bf16[1024,512]{1,0:T(8,128)(2,1)} fusion(bf16[2176,512]{1,0:T(8,128)(2,1)S(1)} %pad_maximum_fusion, s32[1024]{0:T(1024)S(1)} %fusion.26), kind=kCustom, calls=%fused_computation.1 | custom fusion | bytes 2101248 | tf_op jit(solution)/shard_map/gather | solution.py:61
  185.7 5.0 %fusion.33 = (f32[1024]{0:T(1024)S(1)}, f32[1024]{0:T(1024)S(1)}, f32[1024,512]{0,1:T(8,128)}) fusion(bf16[1,512,512]{2,1,0:T(8,128)(2,1)} %all-gather.3, bf16[1024,512]{1,0:T(8,128)(2,1)} %gather_fusion.2, bf16[1024,512]{1,0:T(8,128)(2,1)} %gather_fusion.1, bf16[1024,512]{1,0:T(8,128)(2,1)} %param.10, bf16[1,1,512,512]{3,2,1,0:T(8,128)(2,1)} %all-gather.2), kind=kOutput, calls=%fused_computation.77 | convolution fusion | flops 1080031232 | bytes 6299648 | tf_op jit(solution)/shard_map/dot_general | solution.py:14
  190.7 2.0 add_convert_fusion.1
  192.7 0.5 copy.15
  193.3 8.1 %scatter_custom_fusion = f32[128,512]{1,0:T(8,128)} fusion(s32[1024]{0:T(1024)} %param.12, f32[1024,512]{1,0:T(8,128)S(1)} %copy.15, f32[]{:T(128)} %constant.13.clone.1), kind=kCustom, calls=%fused_computation.56 | custom fusion | flops 524288 | bytes 262656 | tf_op jit(solution)/shard_map/scatter-add | solution.py:78
  201.4 1.8 fusion.35
  203.2 0.1 add_convert_fusion.3
  203.4 1.3 convolution_convert_fusion.1
  204.6 9.2 %gather_fusion.3 = bf16[2048,512]{1,0:T(8,128)(2,1)} fusion(bf16[128,512]{1,0:T(8,128)(2,1)S(1)} %convolution_convert_fusion.1, s32[2048]{0:T(1024)S(1)} %broadcast_clamp_fusion), kind=kCustom, calls=%fused_computation.3 | custom fusion | bytes 4202496 | tf_op jit(solution)/shard_map/gather | solution.py:56
  213.8 8.9 %all-to-all-start.1 = ((bf16[128,16,512]{2,1,0:T(8,128)(2,1)}), bf16[128,16,512]{2,1,0:T(8,128)(2,1)S(1)}, u32[]{:S(2)}, u32[]{:S(2)}) async-start(bf16[128,16,512]{2,1,0:T(8,128)(2,1)} %bitcast.12), calls=%async_computation.1 | async-start | bytes 4194304 | tf_op jit(solution)/shard_map/all_to_all | solution.py:57
  222.7 42.4 %all-gather.7 = bf16[1,1,512,512]{3,2,1,0:T(8,128)(2,1)} all-gather(bf16[1,1,32,512]{3,2,1,0:T(8,128)(2,1)S(1)} %copy-done.8), channel_id=9, replica_groups=mesh['mesh'=8,'chan'=16] {'chan'}, dimensions={2}, use_global_device_ids=true | all-gather | bytes 557056 | tf_op jit(solution)/shard_map/all_gather | solution.py:67
  265.2 24.4 %all-gather.8 = bf16[1,512,512]{2,1,0:T(8,128)(2,1)} all-gather(bf16[1,32,512]{2,1,0:T(8,128)(2,1)S(1)} %copy-done.9), channel_id=10, replica_groups=mesh['mesh'=8,'chan'=16] {'chan'}, dimensions={1}, use_global_device_ids=true | all-gather | bytes 557056 | tf_op jit(solution)/shard_map/all_gather | solution.py:73
  289.6 24.6 %all-gather.9 = bf16[1,512,512]{2,1,0:T(8,128)(2,1)} all-gather(bf16[1,32,512]{2,1,0:T(8,128)(2,1)S(1)} %copy-done.10), channel_id=11, replica_groups=mesh['mesh'=8,'chan'=16] {'chan'}, dimensions={1}, use_global_device_ids=true | all-gather | bytes 557056 | tf_op jit(solution)/shard_map/all_gather | solution.py:94
  314.2 1.3 convolution_convert_fusion
  315.5 5.1 %gather_fusion.5 = bf16[1024,512]{1,0:T(8,128)(2,1)} fusion(bf16[128,512]{1,0:T(8,128)(2,1)S(1)} %convolution_convert_fusion, s32[1024]{0:T(1024)S(1)} %fusion.27), kind=kCustom, calls=%fused_computation.5 | custom fusion | bytes 2101248 | tf_op jit(solution)/shard_map/gather | solution.py:61
  320.5 2.0 fusion.4
  322.5 1.3 copy-done.1
  323.9 1.7 pad_maximum_fusion.1
  325.6 5.1 %gather_fusion.4 = bf16[1024,512]{1,0:T(8,128)(2,1)} fusion(bf16[2176,512]{1,0:T(8,128)(2,1)S(1)} %pad_maximum_fusion.1, s32[1024]{0:T(1024)S(1)} %fusion.26), kind=kCustom, calls=%fused_computation.4 | custom fusion | bytes 2101248 | tf_op jit(solution)/shard_map/gather | solution.py:61
  330.7 4.8 %fusion.32 = (f32[1024]{0:T(1024)S(1)}, f32[1024]{0:T(1024)S(1)}, f32[1024,512]{0,1:T(8,128)}) fusion(bf16[1,512,512]{2,1,0:T(8,128)(2,1)} %all-gather.8, bf16[1024,512]{1,0:T(8,128)(2,1)} %gather_fusion.5, bf16[1024,512]{1,0:T(8,128)(2,1)} %gather_fusion.4, bf16[1024,512]{0,1:T(8,128)(2,1)S(1)} %add_convert_fusion.1, bf16[1,1,512,512]{3,2,1,0:T(8,128)(2,1)} %all-gather.7), kind=kOutput, calls=%fused_computation.76 | convolution fusion | flops 1080031232 | bytes 6299648 | tf_op jit(solution)/shard_map/dot_general | solution.py:14
  335.5 2.0 add_convert_fusion
  337.5 1.6 copy.16
  339.1 1.3 copy.17
  340.4 7.9 %scatter_custom_fusion.1 = f32[128,512]{1,0:T(8,128)S(1)} fusion(s32[1024]{0:T(1024)} %param.12, f32[1024,512]{1,0:T(8,128)} %copy.16, f32[]{:T(128)} %constant.13.clone.1), kind=kCustom, calls=%fused_computation.54 | custom fusion | flops 524288 | bytes 262656 | tf_op jit(solution)/shard_map/scatter-add | solution.py:78
  348.3 0.5 fusion.34
  348.9 0.8 add_convert_fusion.2
  (45 shorter events, 0.3 us)
Async XLA Ops:
  7.2 48.9 %all-gather.17.cloned.1.call-start = ((), (), s32[]{:S(2)}) async-start(), calls=%async_computation.3 | async-start | bytes 1114112 | tf_op jit(solution)/shard_map/all_gather | solution.py:52
  8.8 166.8 %all-gather.15.cloned.1.call-start = ((), (), s32[]{:S(2)}) async-start(), calls=%async_computation.2 | async-start | bytes 1114112 | tf_op jit(solution)/shard_map/all_gather | solution.py:88
  10.4 193.0 %all-gather.21.cloned.1.call-start = ((), (), s32[]{:S(2)}) async-start(), calls=%async_computation.5 | async-start | bytes 1114112 | tf_op jit(solution)/shard_map/all_gather | solution.py:52
  66.6 110.9 %all-to-all-start = ((bf16[128,16,512]{2,1,0:T(8,128)(2,1)}), bf16[128,16,512]{2,1,0:T(8,128)(2,1)S(1)}, u32[]{:S(2)}, u32[]{:S(2)}) async-start(bf16[128,16,512]{2,1,0:T(8,128)(2,1)} %bitcast.3), calls=%async_computation | async-start | bytes 4194304 | tf_op jit(solution)/shard_map/all_to_all | solution.py:57
  74.5 43.2 %copy-start.11 = (bf16[2,32,512]{2,1,0:T(8,128)(2,1)S(1)}, bf16[2,32,512]{2,1,0:T(8,128)(2,1)}, u32[]{:S(2)}) copy-start(bf16[2,32,512]{2,1,0:T(8,128)(2,1)} %param.15) | copy-start | bytes 196612
  74.5 246.0 %all-gather.19.cloned.1.call-start = ((), (), s32[]{:S(2)}) async-start(), calls=%async_computation.4 | async-start | bytes 1114112 | tf_op jit(solution)/shard_map/all_gather | solution.py:88
  75.1 94.0 %copy-start.12 = (s32[1024]{0:T(1024)S(1)}, s32[1024]{0:T(1024)}, u32[]{:S(2)}) copy-start(s32[1024]{0:T(1024)} %param.11) | copy-start | bytes 12292
  75.1 94.0 %copy-start.13 = (s32[1024]{0:T(1024)S(1)}, s32[1024]{0:T(1024)}, u32[]{:S(2)}) copy-start(s32[1024]{0:T(1024)} %param.12) | copy-start | bytes 12292
  75.1 94.0 %copy-start.3 = (bf16[128,512]{1,0:T(8,128)(2,1)S(1)}, bf16[128,512]{1,0:T(8,128)(2,1)}, u32[]{:S(2)}) copy-start(bf16[128,512]{1,0:T(8,128)(2,1)} %param.9) | copy-start | bytes 393220
  177.5 1.3 copy-start
  192.7 8.7 %copy-start.6 = (f32[128,512]{1,0:T(8,128)S(1)}, f32[128,512]{1,0:T(8,128)}, u32[]{:S(2)}) copy-start(f32[128,512]{1,0:T(8,128)} %fusion.5) | copy-start | bytes 786436
  193.3 9.9 %copy-start.4 = (bf16[128,512]{1,0:T(8,128)(2,1)S(1)}, bf16[128,512]{1,0:T(8,128)(2,1)}, u32[]{:S(2)}) copy-start(bf16[128,512]{1,0:T(8,128)(2,1)} %param.9) | copy-start | bytes 393220
  213.8 8.9 %copy-start.8 = (bf16[1,1,32,512]{3,2,1,0:T(8,128)(2,1)S(1)}, bf16[1,1,32,512]{3,2,1,0:T(8,128)(2,1)}, u32[]{:S(2)}) copy-start(bf16[1,1,32,512]{3,2,1,0:T(8,128)(2,1)} %get-tuple-element.14) | copy-start | bytes 98308
  213.8 51.3 %copy-start.9 = (bf16[1,32,512]{2,1,0:T(8,128)(2,1)S(1)}, bf16[1,32,512]{2,1,0:T(8,128)(2,1)}, u32[]{:S(2)}) copy-start(bf16[1,32,512]{2,1,0:T(8,128)(2,1)} %get-tuple-element.20) | copy-start | bytes 98308
  213.8 75.7 %copy-start.10 = (bf16[1,32,512]{2,1,0:T(8,128)(2,1)S(1)}, bf16[1,32,512]{2,1,0:T(8,128)(2,1)}, u32[]{:S(2)}) copy-start(bf16[1,32,512]{2,1,0:T(8,128)(2,1)} %get-tuple-element.23) | copy-start | bytes 98308
  213.8 108.7 %all-to-all-start.1 = ((bf16[128,16,512]{2,1,0:T(8,128)(2,1)}), bf16[128,16,512]{2,1,0:T(8,128)(2,1)S(1)}, u32[]{:S(2)}, u32[]{:S(2)}) async-start(bf16[128,16,512]{2,1,0:T(8,128)(2,1)} %bitcast.12), calls=%async_computation.1 | async-start | bytes 4194304 | tf_op jit(solution)/shard_map/all_to_all | solution.py:57
  322.5 1.3 copy-start.1
  337.4 10.9 %copy-start.2 = (bf16[1,512,512]{2,1,0:T(8,128)(2,1)S(1)}, bf16[1,512,512]{2,1,0:T(8,128)(2,1)}, u32[]{:S(2)}) copy-start(bf16[1,512,512]{2,1,0:T(8,128)(2,1)} %all-gather.9) | copy-start | bytes 1572868
  337.4 10.9 %copy-start.5 = (f32[128,512]{1,0:T(8,128)S(1)}, f32[128,512]{1,0:T(8,128)}, u32[]{:S(2)}) copy-start(f32[128,512]{1,0:T(8,128)} %fusion.4) | copy-start | bytes 786436
  337.4 10.9 %copy-start.7 = (bf16[1,2,512,512]{3,2,1,0:T(8,128)(2,1)S(1)}, bf16[1,2,512,512]{3,2,1,0:T(8,128)(2,1)}, u32[]{:S(2)}) copy-start(bf16[1,2,512,512]{3,2,1,0:T(8,128)(2,1)} %all-gather.19.cloned.1.call-done) | copy-start | bytes 3145732
Sparse Core Ops, SparseCore 0:
  10.7 45.3 all-gather.16
  58.2 60.3 all-gather.14
  120.8 41.9 all-gather.20
  165.3 41.9 all-gather.18
where the time goes:
time: 360 us; the launch traced here: 356 us
  blocking collectives  180 us (50%)
  local copies, waits for them, and re-layouts  53.7 us (15%)
  waiting for transfers between devices  45.3 us (13%)
  other arithmetic  24.4 us (7%)
  matrix products  21.3 us (6%)
  starting transfers between devices  16.9 us (5%)
  between operations  14.1 us (4%)
    all_gather x2, blocking collectives, local(): lax.all_gather(edge_in[round_index, 0], 'chan', axis=0, tiled=True)  82 us
    all_gather x2, blocking collectives, local(): lax.all_gather(node_out[round_index], 'chan', axis=0, tiled=True)  49.6 us
    all_gather x2, blocking collectives, local(): lax.all_gather(edge_out[round_index], 'chan', axis=0, tiled=True)  48.8 us
    all_gather x2, waiting for transfers between devices, local(): lax.all_gather(edge_in[round_index, 1:3], 'chan', axis=1, tiled=True)  44.1 us
    gather x2, local copies, waits for them, and re-layouts, local(): outgoing = send_proj[flat_rows]  18.4 us
    all_to_all x2, starting transfers between devices, local(): lax.all_to_all(outgoing, ('mesh', 'chan'), split_axis=0, concat_axis=0, t...  16.8 us
    scatter-add x2, other arithmetic, local(): jax.ops.segment_sum(edge_state.astype(jnp.float32), receiver_node, num_se...  16 us
    dot_general x4, matrix products, make_adder(): return total + jnp.dot(left, piece, preferred_element_type=jnp.float32)  12.2 us
  transfers between devices with their start and end apart: 6, of which 1 were waited for; matrix products, arithmetic and copies ran while one was open for 19% of the time, Pallas kernels for 0%

commit v1 on v0

v1 whole, which is shorter than its diff:
```python
import functools

import jax
import jax.numpy as jnp
from jax import lax
from jax.experimental import pallas as pl
from jax.experimental.pallas import tpu as pltpu
from jax.sharding import PartitionSpec as P

MESH = pl.DeviceIdType.MESH
F32 = jnp.float32
BF16 = jnp.bfloat16
WIDTH = 512
NODE = 128
EDGE = 1024
DEVICES = 128
SLOT = 16
TILE = 512
GROUPS = ((0, 4), (4, 7))


def mm(a, b):
    return jnp.dot(a, b, preferred_element_type=F32)


def norm_rows(v):
    mean = jnp.sum(v, axis=1, keepdims=True) * (1.0 / WIDTH)
    square = jnp.sum(v * v, axis=1, keepdims=True) * (1.0 / WIDTH)
    return (v - mean) * lax.rsqrt(square - mean * mean + 1e-05)


def silu(v):
    return v / (1.0 + jnp.exp(-v))


def kernel(
    node_ref, edge_ref, sender_ref, receiver_ref, rows_ref, ein, eout, nin, nout,
    node_out_ref, edge_out_ref,
    weights, outgoing, table, pick_sender, pick_receiver, sum_receiver, pick_send, base, aggregate,
    ready, load_sem, ex_send, ex_recv, p1s, p1r, p2s, p2r, d1s, d1r, d2s, d2r,
):
    m = lax.axis_index("mesh")
    c = lax.axis_index("chan")
    me = m * 16 + c
    x, core = m // 2, lax.rem(m, 2)
    z, y = c // 4, lax.rem(c, 4)
    sibling = (x * 2 + 1 - core, c)

    barrier = pltpu.get_barrier_semaphore()

    def greet_line(k, carry):
        pl.semaphore_signal(barrier, inc=1, device_id=(lax.rem(m + k, 8), c), device_id_type=MESH)
        return carry

    def greet_plane(sem):
        def step(k, carry):
            pl.semaphore_signal(sem, inc=1, device_id=(m, lax.rem(c + k, 16)), device_id_type=MESH)
            return carry
        lax.fori_loop(1, 16, step, 0)

    lax.fori_loop(1, 8, greet_line, 0)
    greet_plane(barrier)

    for r in range(2):
        for src, low, high in ((ein.at[r], 0, 3), (eout.at[pl.ds(r, 1)], 3, 4), (nin.at[r], 4, 6), (nout.at[pl.ds(r, 1)], 6, 7)):
            pltpu.make_async_copy(src, weights.at[r, low:high, z, y], load_sem.at[r]).start()

    sub = lax.broadcasted_iota(jnp.int32, (128, 128), 0)
    lane = lax.broadcasted_iota(jnp.int32, (128, 128), 1)
    lane_f = lane.astype(F32)
    eye = sub == lane
    ones = jnp.ones((128, 128), BF16)

    def column(row):
        wide = jnp.broadcast_to(row.astype(F32), (128, 128))
        return mm(jnp.where(eye, wide, 0.0).astype(BF16), ones)

    def hot(mask):
        return jnp.where(mask, 1.0, 0.0).astype(BF16)

    slots = rows_ref[...].astype(F32).astype(BF16)

    def send_block(b, carry):
        spread = mm(hot(lane == 8 * b + sub // SLOT), slots)
        at = lax.broadcasted_iota(jnp.int32, (128, SLOT), 1) == lax.rem(lax.broadcasted_iota(jnp.int32, (128, SLOT), 0), SLOT)
        index = jnp.sum(jnp.where(at, spread, 0.0), axis=1, keepdims=True)
        pick = hot(index == lane_f)
        rows = pl.ds(pl.multiple_of(b * 128, 128), 128)
        pick_send[rows, :] = pick
        outgoing[rows, :] = mm(pick, node_ref[...]).astype(BF16)
        return carry

    lax.fori_loop(0, 16, send_block, 0)
    table[0, pl.ds(pl.multiple_of(me * SLOT, SLOT), SLOT), :] = jnp.zeros((SLOT, WIDTH), BF16)
    table[1, pl.ds(pl.multiple_of(me * SLOT, SLOT), SLOT), :] = jnp.zeros((SLOT, WIDTH), BF16)

    def wait_load(r):
        pltpu.make_async_copy(weights.at[r, :, z, y], weights.at[r, :, z, y], load_sem.at[r]).wait()

    def remote(src, send, recv, device):
        return pltpu.make_async_remote_copy(
            src_ref=src, dst_ref=src, send_sem=send, recv_sem=recv, device_id=device, device_id_type=MESH
        )

    def at(pos, k):
        return lax.rem(pos + k + 4, 4)

    def phase1(r, g, k):
        low, high = GROUPS[g]
        to = (m, 4 * z + at(y, k)) if g == 0 else (m, 4 * at(z, k) + y)
        return remote(weights.at[r, low:high, z, y, core], p1s.at[r, g, k - 1], p1r.at[r, g, k - 1], to)

    def side1(r, g, k):
        low, high = GROUPS[g]
        if g == 0:
            src = weights.at[r, low:high, z, at(y, -k), core]
        else:
            src = weights.at[r, low:high, at(z, -k), y, core]
        return remote(src, d1s.at[r, g, k - 1], d1r.at[r, g, k - 1], sibling)

    def phase2(r, g, k):
        low, high = GROUPS[g]
        if g == 0:
            return remote(weights.at[r, low:high, z, :, core], p2s.at[r, g, k - 1], p2r.at[r, g, k - 1], (m, 4 * at(z, k) + y))
        return remote(weights.at[r, low:high, :, y, core], p2s.at[r, g, k - 1], p2r.at[r, g, k - 1], (m, 4 * z + at(y, k)))

    def side2(r, g, k):
        low, high = GROUPS[g]
        if g == 0:
            src = weights.at[r, low:high, at(z, -k), :, core]
        else:
            src = weights.at[r, low:high, :, at(y, -k), core]
        return remote(src, d2s.at[r, g, k - 1], d2r.at[r, g, k - 1], sibling)

    def start_phase1(r):
        wait_load(r)
        for g in range(2):
            for k in (1, 3, 2):
                phase1(r, g, k).start()

    def start_phase2(r):
        for g in range(2):
            for k in (1, 2, 3):
                phase1(r, g, k).wait_recv()
            for k in (1, 3, 2):
                phase2(r, g, k).start()
            for k in (1, 2, 3):
                side1(r, g, k).start()

    def start_side2(r):
        for g in range(2):
            for k in (1, 2, 3):
                phase2(r, g, k).wait_recv()
                side2(r, g, k).start()

    def wait_side(r, g):
        for k in (1, 2, 3):
            side1(r, g, k).wait_recv()
            side2(r, g, k).wait_recv()

    def start_exchange(r):
        def step(k, carry):
            p = lax.rem(me + k, DEVICES)
            pltpu.make_async_remote_copy(
                src_ref=outgoing.at[pl.ds(pl.multiple_of(p * SLOT, SLOT), SLOT)],
                dst_ref=table.at[r, pl.ds(pl.multiple_of(me * SLOT, SLOT), SLOT)],
                send_sem=ex_send.at[r], recv_sem=ex_recv.at[r],
                device_id=(p // 16, lax.rem(p, 16)), device_id_type=MESH,
            ).start()
            return carry
        lax.fori_loop(1, DEVICES, step, 0)

    def exchange_bytes(sem):
        part = pl.ds(0, (DEVICES - 1) * SLOT)
        return pltpu.make_async_copy(outgoing.at[part], outgoing.at[part], sem)

    def matrix(r, i):
        return weights[r, i].reshape(WIDTH, WIDTH)

    pl.semaphore_wait(barrier, 22)
    greet_plane(ready)
    start_phase1(0)

    def edge_block(i, carry):
        rows = pl.ds(pl.multiple_of(i * 128, 128), 128)
        sender = sender_ref[pl.ds(i, 1), :]
        receiver = receiver_ref[pl.ds(i, 1), :]
        index = column(lax.shift_right_logical(sender, 7)) * 128.0 + column(sender & 127)
        for j in range(17):
            pick_sender[rows, j * 128:(j + 1) * 128] = hot(index == lane_f + 128.0 * j)
        pick_receiver[rows, :] = hot(column(receiver) == lane_f)
        sum_receiver[:, rows] = hot(receiver == sub)
        return carry

    pl.semaphore_wait(ready, 15)
    start_exchange(0)
    lax.fori_loop(0, 8, edge_block, 0)
    start_phase2(0)
    start_side2(0)
    start_phase1(1)

    for r in range(2):
        nodes = node_ref if r == 0 else node_out_ref
        edges = edge_ref if r == 0 else edge_out_ref
        wait_side(r, 0)

        recv_proj = mm(nodes[...], matrix(r, 2)).astype(BF16)

        def before(t, carry):
            rows = pl.ds(pl.multiple_of(t * TILE, TILE), TILE)
            base[rows, :] = mm(edges[rows, :], matrix(r, 0)) + mm(pick_receiver[rows, :], recv_proj)
            return carry

        lax.fori_loop(0, EDGE // TILE, before, 0)
        exchange_bytes(ex_recv.at[r]).wait()
        if r == 0:
            start_phase2(1)

        def after(t, carry):
            rows = pl.ds(pl.multiple_of(t * TILE, TILE), TILE)
            gathered = mm(pick_sender[rows, 0:128], nodes[...]) + mm(pick_sender[rows, 128:2176], table[r])
            preact = base[rows, :] + mm(gathered.astype(BF16), matrix(r, 1))
            output = mm(silu(preact).astype(BF16), matrix(r, 3))
            edge_out_ref[rows, :] = (edges[rows, :].astype(F32) + norm_rows(output)).astype(BF16)
            return carry

        lax.fori_loop(0, EDGE // TILE, after, 0)
        if r == 0:
            start_side2(1)
        wait_side(r, 1)
        total = mm(sum_receiver[...], edge_out_ref[...]).astype(BF16)
        preact = mm(nodes[...], matrix(r, 4)) + mm(total, matrix(r, 5))
        output = mm(silu(preact).astype(BF16), matrix(r, 6))
        node_out_ref[...] = (nodes[...].astype(F32) + norm_rows(output)).astype(BF16)
        exchange_bytes(ex_send.at[r]).wait()
        if r == 0:
            def resend(b, carry):
                rows = pl.ds(pl.multiple_of(b * 512, 512), 512)
                outgoing[rows, :] = mm(pick_send[rows, :], node_out_ref[...]).astype(BF16)
                return carry
            lax.fori_loop(0, 4, resend, 0)
            start_exchange(1)

    for r in range(2):
        for g in range(2):
            for k in (1, 2, 3):
                phase1(r, g, k).wait_send()
                phase2(r, g, k).wait_send()
                side1(r, g, k).wait_send()
                side2(r, g, k).wait_send()


def local(node_latents, edge_latents, sender_slot, receiver_node, send_rows, edge_in, edge_out, node_in, node_out):
    vmem = pl.BlockSpec(memory_space=pltpu.VMEM)
    anywhere = pl.BlockSpec(memory_space=pl.ANY)
    dma = pltpu.SemaphoreType.DMA
    return pl.pallas_call(
        kernel,
        out_shape=(
            jax.ShapeDtypeStruct((NODE, WIDTH), BF16),
            jax.ShapeDtypeStruct((EDGE, WIDTH), BF16),
        ),
        in_specs=[vmem] * 5 + [anywhere] * 4,
        out_specs=(vmem, vmem),
        scratch_shapes=[
            pltpu.VMEM((2, 7, 4, 4, 2, 16, WIDTH), BF16),
            pltpu.VMEM((DEVICES * SLOT, WIDTH), BF16),
            pltpu.VMEM((2, DEVICES * SLOT, WIDTH), BF16),
            pltpu.VMEM((EDGE, NODE + DEVICES * SLOT), BF16),
            pltpu.VMEM((EDGE, NODE), BF16),
            pltpu.VMEM((NODE, EDGE), BF16),
            pltpu.VMEM((DEVICES * SLOT, NODE), BF16),
            pltpu.VMEM((EDGE, WIDTH), F32),
            pltpu.VMEM((NODE, WIDTH), F32),
            pltpu.SemaphoreType.REGULAR,
            dma((2,)), dma((2,)), dma((2,)),
        ] + [dma((2, 2, 3))] * 8,
        compiler_params=pltpu.CompilerParams(
            collective_id=0, has_side_effects=True, vmem_limit_bytes=56 * 1024 * 1024
        ),
    )(
        node_latents,
        edge_latents,
        sender_slot.reshape(8, 128),
        receiver_node.reshape(8, 128),
        send_rows,
        edge_in.reshape(2, 3, 2, 16, WIDTH),
        edge_out.reshape(2, 2, 16, WIDTH),
        node_in.reshape(2, 2, 2, 16, WIDTH),
        node_out.reshape(2, 2, 16, WIDTH),
    )


def solution(mesh):
    rows = P(("mesh", "chan"), None)
    flat = P(("mesh", "chan"))
    return jax.shard_map(
        local,
        mesh=mesh,
        in_specs=(
            rows, rows, flat, flat, rows,
            P(None, None, "chan", None), P(None, "chan", None),
            P(None, None, "chan", None), P(None, "chan", None),
        ),
        out_specs=(rows, rows),
        check_vma=False,
    )
```

time: 360 us -> 115 us (0.32)
  blocking collectives: 180 us -> 0 us
  Pallas kernels: 0 us -> 108 us
  local copies, waits for them, and re-layouts: 53.7 us -> 5.25 us
  waiting for transfers between devices: 45.3 us -> 0 us
  other arithmetic: 24.4 us -> 0 us
  matrix products: 21.3 us -> 0 us
  starting transfers between devices: 16.9 us -> 0 us
  between operations: 14.1 us -> 0.65 us
    all_gather x6 -> x0, blocking collectives: 180 us -> none  [the longest x2 82 us: local(): lax.all_gather(edge_in[round_index, 0], 'chan', axis=0, tiled=True)]
    pallas_call x0 -> x1, Pallas kernels: none -> 108 us  [local(): pl.pallas_call(kernel, out_shape=(jax.ShapeDtypeStruct((NODE, WIDTH), BF1...]
    all_gather x4 -> x0, waiting for transfers between devices: 44.1 us -> none  [the longest x2 44.1 us: local(): lax.all_gather(edge_in[round_index, 1:3], 'chan', axis=1, tiled=True)]
    gather x6 -> x0, local copies, waits for them, and re-layouts: 38.6 us -> none  [the longest x2 18.4 us: local(): outgoing = send_proj[flat_rows]]
    dot_general x10 -> x0, matrix products: 21.3 us -> none  [the longest x4 12.2 us: make_adder(): return total + jnp.dot(left, piece, preferred_element_type=jnp.float32)]
    all_to_all x2 -> x0, starting transfers between devices: 16.8 us -> none  [local(): lax.all_to_all(outgoing, ('mesh', 'chan'), split_axis=0, concat_axis=0, t...]
    scatter-add x2 -> x0, other arithmetic: 16 us -> none  [local(): jax.ops.segment_sum(edge_state.astype(jnp.float32), receiver_node, num_se...]
    slice x5 -> x0, local copies, waits for them, and re-layouts: 6.43 us -> none  [the longest x1 1.53 us: local(): edge_in[round_index, 1:3]]
  transfers between devices with their start and end apart: 6 -> 0, of which waited for: 1 -> 0; matrix products, arithmetic and copies ran while one was open for 19% -> 0% of each run, Pallas kernels for 0% -> 0%
where the time goes in v1:
time: 115 us; the launch traced here: 114 us
  Pallas kernels  108 us (94%)
  local copies, waits for them, and re-layouts  5.25 us (5%)
    pallas_call x1, Pallas kernels, local(): pl.pallas_call(kernel, out_shape=(jax.ShapeDtypeStruct((NODE, WIDTH), BF1...  108 us
    unnamed x5, local copies, waits for them, and re-layouts  5.25 us

profile of v1, /device:TPU:0, one launch (start us, length us, event | category | flops | bytes accessed | tf_op | source)
XLA Modules:
  0.0 113.6 jit_solution(14865508393720597598)
XLA Ops:
  0.6 0.0 copy-start
  0.6 0.7 copy-done
  1.3 0.7 copy.11.rows_ref
  2.1 107.7 %shard_map.104 = (bf16[128,512]{1,0:T(8,128)(2,1)}, bf16[1024,512]{1,0:T(8,128)(2,1)}) custom-call(bf16[128,512]{1,0:T(8,128)(2,1)} %node_ref.1, bf16[1024,512]{1,0:T(8,128)(2,1)} %edge_ref.1, s32[8,128]{1,0:T(8,128)} %bitcast.10, s32[8,128]{1,0:T(8,128)} %bitcast.11, s32[128,16]{1,0:T(8,128)} %copy.11.rows_ref, bf16[2,3,2,16,512]{4,3,2,1,0:T(8,128)(2,1)} %bitcast.6, ...), custom_call_target="tpu_custom_call" | custom-call | tf_op jit(solution)/shard_map/pallas_call | solution.py:257
  109.8 1.6 %copy.14 = bf16[128,512]{1,0:T(8,128)(2,1)} copy(bf16[128,512]{1,0:T(8,128)(2,1)} %get-tuple-element.4) | data formatting | bytes 262144
  111.3 2.3 %copy.15 = bf16[1024,512]{1,0:T(8,128)(2,1)} copy(bf16[1024,512]{1,0:T(8,128)(2,1)} %get-tuple-element.5) | data formatting | bytes 2097152
Async XLA Ops:
  0.6 0.7 copy-start

commit v2 on v1

v2 whole, which is shorter than its diff:
```python
import jax
import jax.numpy as jnp
from jax import lax
from jax.experimental import pallas as pl
from jax.experimental.pallas import tpu as pltpu
from jax.sharding import PartitionSpec as P

MESH = pl.DeviceIdType.MESH
F32 = jnp.float32
BF16 = jnp.bfloat16
WIDTH = 512
NODE = 128
EDGE = 1024
SLOT = 16
PLANE = 32
PLANE_ROWS = PLANE * SLOT
TILE = 512
PARTS = ((0, 4), (4, 7))
ORDER = (1, 3, 2)


def mm(a, b):
    return jnp.dot(a, b, preferred_element_type=F32)


def hot(mask):
    return jnp.where(mask, 1.0, 0.0).astype(BF16)


def norm_rows(v):
    mean = jnp.sum(v, axis=1, keepdims=True) * (1.0 / WIDTH)
    square = jnp.sum(v * v, axis=1, keepdims=True) * (1.0 / WIDTH)
    return (v - mean) * lax.rsqrt(square - mean * mean + 1e-05)


def silu(v):
    return v / (1.0 + jnp.exp(-v))


def kernel(
    node_ref, edge_ref, sender_ref, receiver_ref, slots_ref, ein, eout, nin, nout,
    node_out_ref, edge_out_ref,
    weights, outgoing, table, node_mid, line_nodes, own_slots, line_slots,
    pick_local, pick_sender, pick_receiver, sum_receiver, pick_send, base, gathered,
    load_sem, ex_send, ex_recv, node_send, node_recv, slot_send, slot_recv,
    plane_send, plane_recv, line_send, line_recv, side_send, side_recv,
):
    m = lax.axis_index("mesh")
    c = lax.axis_index("chan")
    x, core = m // 2, lax.rem(m, 2)
    own = core * 16 + c
    sibling = (x * 2 + 1 - core, c)

    def along(k):
        return lax.rem(x + k + 4, 4)

    def line(k):
        return (along(k) * 2 + core, c)

    def peer(j):
        q = lax.rem(own + j, PLANE)
        return q, (x * 2 + q // 16, lax.rem(q, 16))

    barrier = pltpu.get_barrier_semaphore()
    for k in ORDER:
        pl.semaphore_signal(barrier, inc=1, device_id=line(k), device_id_type=MESH)

    def greet(j, carry):
        pl.semaphore_signal(barrier, inc=1, device_id=peer(j)[1], device_id_type=MESH)
        return carry

    lax.fori_loop(1, PLANE, greet, 0)

    columns = pl.ds(pl.multiple_of(x * 128, 128), 128)
    for r in range(2):
        for src, low, high in (
            (ein.at[r, :, core, :, columns], 0, 3),
            (eout.at[pl.ds(r, 1), core, :, columns], 3, 4),
            (nin.at[r, :, core, :, columns], 4, 6),
            (nout.at[pl.ds(r, 1), core, :, columns], 6, 7),
        ):
            pltpu.make_async_copy(src, weights.at[r, x, c, core, low:high], load_sem.at[r]).start()

    def remote(src, dst, send, recv, device):
        return pltpu.make_async_remote_copy(
            src_ref=src, dst_ref=dst, send_sem=send, recv_sem=recv, device_id=device, device_id_type=MESH
        )

    def wait_load(r):
        ref = weights.at[r, x, c, core]
        pltpu.make_async_copy(ref, ref, load_sem.at[r]).wait()

    def start_plane(r):
        wait_load(r)

        def step(j, carry):
            ref = weights.at[r, x, c, core]
            remote(ref, ref, plane_send.at[r], plane_recv.at[r], (m, lax.rem(c + j, 16))).start()
            return carry
        lax.fori_loop(1, 16, step, 0)

    def plane_bytes(r, sem):
        ref = weights.at[r, x, 0:15, core]
        return pltpu.make_async_copy(ref, ref, sem.at[r])

    def line_copy(r, part, k):
        low, high = PARTS[part]
        ref = weights.at[r, x, :, core, low:high]
        return remote(ref, ref, line_send.at[r, part, k - 1], line_recv.at[r, part, k - 1], line(k))

    def side_copy(r, part, k):
        low, high = PARTS[part]
        ref = weights.at[r, along(-k), :, core, low:high]
        return remote(ref, ref, side_send.at[r, part, k], side_recv.at[r, part, k], sibling)

    def start_line(r):
        plane_bytes(r, plane_recv).wait()
        for part in range(2):
            for k in ORDER:
                line_copy(r, part, k).start()
            side_copy(r, part, 0).start()

    def start_side(r, part):
        for k in ORDER:
            line_copy(r, part, k).wait_recv()
            side_copy(r, part, k).start()

    def wait_side(r, part):
        for k in range(4):
            side_copy(r, part, k).wait_recv()

    def matrix(r, i):
        return jnp.concatenate([weights[r, b, :, :, i].reshape(WIDTH, 128) for b in range(4)], axis=1)

    def slot_copy(k):
        src = own_slots.at[pl.ds(pl.multiple_of(along(k) * PLANE, PLANE), PLANE)]
        return remote(src, line_slots.at[k], slot_send.at[k - 1], slot_recv.at[k - 1], line(k))

    def node_copy(r, k):
        src = node_ref if r == 0 else node_mid
        return remote(src, line_nodes.at[r, k - 1], node_send.at[r, k - 1], node_recv.at[r, k - 1], line(k))

    sub = lax.broadcasted_iota(jnp.int32, (128, 128), 0)
    lane = lax.broadcasted_iota(jnp.int32, (128, 128), 1)
    lane_f = lane.astype(F32)
    at_slot = lane == lax.rem(sub, SLOT)

    def make_pick(k):
        def step(b, carry):
            which = lax.broadcasted_iota(jnp.int32, (128, PLANE), 1)
            row = lax.broadcasted_iota(jnp.int32, (128, PLANE), 0)
            spread = mm(hot(which == 8 * b + row // SLOT), line_slots[k])
            index = jnp.sum(jnp.where(at_slot, spread, 0.0), axis=1, keepdims=True)
            pick_send[k, pl.ds(pl.multiple_of(b * 128, 128), 128), :] = hot(index == lane_f)
            return carry
        lax.fori_loop(0, 4, step, 0)

    def gather(r, k):
        if k:
            nodes = line_nodes[r, k - 1]
        else:
            nodes = node_ref[...] if r == 0 else node_mid[...]
        outgoing[k] = mm(pick_send[k], nodes).astype(BF16)

    def landing(r, k):
        at = ((along(-k) * 2 + core) * 16 + c) * SLOT
        return table.at[r, pl.ds(pl.multiple_of(at, SLOT), SLOT)]

    def send(r, k):
        def step(j, carry):
            q, device = peer(j)
            src = outgoing.at[k, pl.ds(pl.multiple_of(q * SLOT, SLOT), SLOT)]
            remote(src, landing(r, k), ex_send.at[r, k], ex_recv.at[r, k], device).start()
            return carry
        lax.fori_loop(1, PLANE, step, 0)
        if k:
            landing(r, k)[...] = outgoing[k, pl.ds(pl.multiple_of(own * SLOT, SLOT), SLOT), :]
        else:
            landing(r, k)[...] = jnp.zeros((SLOT, WIDTH), BF16)

    def exchange_bytes(sem):
        ref = outgoing.at[0, pl.ds(0, (PLANE - 1) * SLOT)]
        return pltpu.make_async_copy(ref, ref, sem)

    slots = jnp.concatenate([slots_ref[...].astype(F32), jnp.zeros((128 - SLOT, 128), F32)], axis=0)
    own_slots[...] = jnp.transpose(slots).astype(BF16)
    line_slots[0] = own_slots[pl.ds(pl.multiple_of(x * PLANE, PLANE), PLANE), :]
    make_pick(0)
    gather(0, 0)

    pl.semaphore_wait(barrier, 34)
    for k in ORDER:
        slot_copy(k).start()
        node_copy(0, k).start()
    start_plane(0)
    send(0, 0)

    eye = sub == lane
    ones = jnp.ones((128, 128), BF16)

    def column(row):
        wide = jnp.broadcast_to(row.astype(F32), (128, 128))
        return mm(jnp.where(eye, wide, 0.0).astype(BF16), ones)

    def edge_block(i, carry):
        rows = pl.ds(pl.multiple_of(i * 128, 128), 128)
        sender = sender_ref[pl.ds(i, 1), :]
        receiver = receiver_ref[pl.ds(i, 1), :]
        index = column(lax.shift_right_logical(sender, 7)) * 128.0 + column(sender & 127)
        pick_local[rows, :] = hot(index == lane_f)
        for j in range(16):
            pick_sender[j // 4, rows, (j % 4) * 128:(j % 4 + 1) * 128] = hot(index == lane_f + 128.0 * (j + 1))
        pick_receiver[rows, :] = hot(column(receiver) == lane_f)
        sum_receiver[:, rows] = hot(receiver == sub)
        return carry

    def relay(r, k):
        if r == 0:
            slot_copy(k).wait_recv()
            make_pick(k)
        node_copy(r, k).wait_recv()
        gather(r, k)
        send(r, k)

    for k in ORDER[:2]:
        relay(0, k)
    start_line(0)
    relay(0, 2)
    start_plane(1)
    lax.fori_loop(0, EDGE // 128, edge_block, 0)
    start_side(0, 0)

    for r in range(2):
        nodes = node_ref if r == 0 else node_mid
        edges = edge_ref if r == 0 else edge_out_ref
        wait_side(r, 0)
        recv_proj = mm(nodes[...], matrix(r, 2)).astype(BF16)

        def before(t, carry):
            rows = pl.ds(pl.multiple_of(t * TILE, TILE), TILE)
            base[rows, :] = mm(edges[rows, :], matrix(r, 0)) + mm(pick_receiver[rows, :], recv_proj)
            gathered[rows, :] = mm(pick_local[rows, :], nodes[...])
            return carry

        lax.fori_loop(0, EDGE // TILE, before, 0)
        start_side(r, 1)
        for k in (0,) + ORDER:
            exchange_bytes(ex_recv.at[r, k]).wait()
            source = along(-k)

            def arrive(t, carry):
                rows = pl.ds(pl.multiple_of(t * TILE, TILE), TILE)
                block = table[r, pl.ds(pl.multiple_of(source * PLANE_ROWS, PLANE_ROWS), PLANE_ROWS), :]
                gathered[rows, :] += mm(pick_sender[source, rows, :], block)
                return carry

            lax.fori_loop(0, EDGE // TILE, arrive, 0)
        if r == 0:
            start_line(1)

        def after(t, carry):
            rows = pl.ds(pl.multiple_of(t * TILE, TILE), TILE)
            preact = base[rows, :] + mm(gathered[rows, :].astype(BF16), matrix(r, 1))
            output = mm(silu(preact).astype(BF16), matrix(r, 3))
            edge_out_ref[rows, :] = (edges[rows, :].astype(F32) + norm_rows(output)).astype(BF16)
            return carry

        lax.fori_loop(0, EDGE // TILE, after, 0)
        wait_side(r, 1)
        total = mm(sum_receiver[...], edge_out_ref[...]).astype(BF16)
        preact = mm(nodes[...], matrix(r, 4)) + mm(total, matrix(r, 5))
        output = mm(silu(preact).astype(BF16), matrix(r, 6))
        result = (nodes[...].astype(F32) + norm_rows(output)).astype(BF16)
        for k in range(4):
            exchange_bytes(ex_send.at[r, k]).wait()
        if r == 0:
            node_mid[...] = result
            for k in ORDER:
                node_copy(1, k).start()
            gather(1, 0)
            send(1, 0)
            for k in ORDER:
                relay(1, k)
            start_side(1, 0)
        else:
            node_out_ref[...] = result

    for r in range(2):
        plane_bytes(r, plane_send).wait()
        for k in ORDER:
            node_copy(r, k).wait_send()
        for part in range(2):
            for k in ORDER:
                line_copy(r, part, k).wait_send()
            for k in range(4):
                side_copy(r, part, k).wait_send()
    for k in ORDER:
        slot_copy(k).wait_send()


def local(node_latents, edge_latents, sender_slot, receiver_node, send_rows, edge_in, edge_out, node_in, node_out):
    vmem = pl.BlockSpec(memory_space=pltpu.VMEM)
    anywhere = pl.BlockSpec(memory_space=pl.ANY)
    dma = pltpu.SemaphoreType.DMA
    return pl.pallas_call(
        kernel,
        out_shape=(
            jax.ShapeDtypeStruct((NODE, WIDTH), BF16),
            jax.ShapeDtypeStruct((EDGE, WIDTH), BF16),
        ),
        in_specs=[vmem] * 5 + [anywhere] * 4,
        out_specs=(vmem, vmem),
        scratch_shapes=[
            pltpu.VMEM((2, 4, 16, 2, 7, 16, 128), BF16),
            pltpu.VMEM((4, PLANE_ROWS, WIDTH), BF16),
            pltpu.VMEM((2, 4 * PLANE_ROWS, WIDTH), BF16),
            pltpu.VMEM((NODE, WIDTH), BF16),
            pltpu.VMEM((2, 3, NODE, WIDTH), BF16),
            pltpu.VMEM((128, 128), BF16),
            pltpu.VMEM((4, PLANE, 128), BF16),
            pltpu.VMEM((EDGE, NODE), BF16),
            pltpu.VMEM((4, EDGE, PLANE_ROWS), BF16),
            pltpu.VMEM((EDGE, NODE), BF16),
            pltpu.VMEM((NODE, EDGE), BF16),
            pltpu.VMEM((4, PLANE_ROWS, NODE), BF16),
            pltpu.VMEM((EDGE, WIDTH), F32),
            pltpu.VMEM((EDGE, WIDTH), F32),
            dma((2,)), dma((2, 4)), dma((2, 4)), dma((2, 3)), dma((2, 3)), dma((3,)), dma((3,)),
            dma((2,)), dma((2,)), dma((2, 2, 3)), dma((2, 2, 3)), dma((2, 2, 4)), dma((2, 2, 4)),
        ],
        compiler_params=pltpu.CompilerParams(
            collective_id=0, has_side_effects=True, vmem_limit_bytes=56 * 1024 * 1024
        ),
    )(
        node_latents,
        edge_latents,
        sender_slot.reshape(8, 128),
        receiver_node.reshape(8, 128),
        jnp.transpose(send_rows),
        edge_in.reshape(2, 3, 2, 16, WIDTH),
        edge_out.reshape(2, 2, 16, WIDTH),
        node_in.reshape(2, 2, 2, 16, WIDTH),
        node_out.reshape(2, 2, 16, WIDTH),
    )


def solution(mesh):
    rows = P(("mesh", "chan"), None)
    flat = P(("mesh", "chan"))
    return jax.shard_map(
        local,
        mesh=mesh,
        in_specs=(
            rows, rows, flat, flat, rows,
            P(None, None, "chan", None), P(None, "chan", None),
            P(None, None, "chan", None), P(None, "chan", None),
        ),
        out_specs=(rows, rows),
        check_vma=False,
    )
```

time: 115 us -> 98.7 us (0.86)
  Pallas kernels: 108 us -> 93.8 us
  local copies, waits for them, and re-layouts: 5.25 us -> 3.83 us
    pallas_call x1, Pallas kernels: 108 us -> 93.8 us  [local(): pl.pallas_call(kernel, out_shape=(jax.ShapeDtypeStruct((NODE, WIDTH), BF1...]
    unnamed x5 -> x2, local copies, waits for them, and re-layouts: 5.25 us -> 3.83 us
where the time goes in v2:
time: 98.7 us; the launch traced here: 98.3 us
  Pallas kernels  93.8 us (95%)
  local copies, waits for them, and re-layouts  3.83 us (4%)
    pallas_call x1, Pallas kernels, local(): pl.pallas_call(kernel, out_shape=(jax.ShapeDtypeStruct((NODE, WIDTH), BF1...  93.8 us
    unnamed x2, local copies, waits for them, and re-layouts  3.83 us

profile of v2, /device:TPU:0, one launch (start us, length us, event | category | flops | bytes accessed | tf_op | source)
XLA Modules:
  0.0 98.3 jit_solution(15075200884337144996)
XLA Ops:
  0.6 93.8 %shard_map.104 = (bf16[128,512]{1,0:T(8,128)(2,1)}, bf16[1024,512]{1,0:T(8,128)(2,1)}) custom-call(bf16[128,512]{1,0:T(8,128)(2,1)} %node_ref.1, bf16[1024,512]{1,0:T(8,128)(2,1)} %edge_ref.1, s32[8,128]{1,0:T(8,128)} %bitcast.12, s32[8,128]{1,0:T(8,128)} %bitcast.13, s32[16,128]{1,0:T(8,128)} %bitcast.11, bf16[2,3,2,16,512]{4,3,2,1,0:T(8,128)(2,1)} %bitcast.7, ...), custom_call_target="tpu_custom_call" | custom-call | tf_op jit(solution)/shard_map/pallas_call | solution.py:305
  94.5 1.6 %copy.13 = bf16[128,512]{1,0:T(8,128)(2,1)} copy(bf16[128,512]{1,0:T(8,128)(2,1)} %get-tuple-element.4) | data formatting | bytes 262144
  96.1 2.3 %copy.14 = bf16[1024,512]{1,0:T(8,128)(2,1)} copy(bf16[1024,512]{1,0:T(8,128)(2,1)} %get-tuple-element.5) | data formatting | bytes 2097152

commit v3 on v2

--- a/solution.py
+++ b/solution.py
@@ -43,7 +43,7 @@
     weights, outgoing, table, node_mid, line_nodes, own_slots, line_slots,
     pick_local, pick_sender, pick_receiver, sum_receiver, pick_send, base, gathered,
     load_sem, ex_send, ex_recv, node_send, node_recv, slot_send, slot_recv,
-    plane_send, plane_recv, line_send, line_recv, side_send, side_recv,
+    plane_send, plane_recv, line_send, line_recv, half_send, half_recv, side_send, side_recv,
 ):
     m = lax.axis_index("mesh")
     c = lax.axis_index("chan")
@@ -108,6 +108,12 @@
         ref = weights.at[r, x, :, core, low:high]
         return remote(ref, ref, line_send.at[r, part, k - 1], line_recv.at[r, part, k - 1], line(k))
 
+    def half_copy(r, part, k):
+        low, high = PARTS[part]
+        half = pl.ds(0, 8) if k == 1 else pl.ds(8, 8)
+        ref = weights.at[r, along(-k), half, core, low:high]
+        return remote(ref, ref, half_send.at[r, part, k - 1], half_recv.at[r, part, k - 1], line(k))
+
     def side_copy(r, part, k):
         low, high = PARTS[part]
         ref = weights.at[r, along(-k), :, core, low:high]
@@ -116,14 +122,21 @@
     def start_line(r):
         plane_bytes(r, plane_recv).wait()
         for part in range(2):
-            for k in ORDER:
+            for k in (1, 3):
                 line_copy(r, part, k).start()
+        for part in range(2):
             side_copy(r, part, 0).start()
 
-    def start_side(r, part):
-        for k in ORDER:
+    def pass_on(r, part):
+        for k in (1, 3):
             line_copy(r, part, k).wait_recv()
+            half_copy(r, part, k).start()
             side_copy(r, part, k).start()
+
+    def finish_line(r, part):
+        for k in (1, 3):
+            half_copy(r, part, k).wait_recv()
+        side_copy(r, part, 2).start()
 
     def wait_side(r, part):
         for k in range(4):
@@ -222,13 +235,17 @@
         gather(r, k)
         send(r, k)
 
-    for k in ORDER[:2]:
-        relay(0, k)
+    start_plane(1)
     start_line(0)
+    relay(0, 1)
+    relay(0, 3)
+    pass_on(0, 0)
     relay(0, 2)
-    start_plane(1)
+    pass_on(0, 1)
+    finish_line(0, 0)
     lax.fori_loop(0, EDGE // 128, edge_block, 0)
-    start_side(0, 0)
+    finish_line(0, 1)
+    start_line(1)
 
     for r in range(2):
         nodes = node_ref if r == 0 else node_mid
@@ -243,7 +260,6 @@
             return carry
 
         lax.fori_loop(0, EDGE // TILE, before, 0)
-        start_side(r, 1)
         for k in (0,) + ORDER:
             exchange_bytes(ex_recv.at[r, k]).wait()
             source = along(-k)
@@ -256,7 +272,7 @@
 
             lax.fori_loop(0, EDGE // TILE, arrive, 0)
         if r == 0:
-            start_line(1)
+            pass_on(1, 0)
 
         def after(t, carry):
             rows = pl.ds(pl.multiple_of(t * TILE, TILE), TILE)
@@ -281,7 +297,9 @@
             send(1, 0)
             for k in ORDER:
                 relay(1, k)
-            start_side(1, 0)
+            finish_line(1, 0)
+            pass_on(1, 1)
+            finish_line(1, 1)
         else:
             node_out_ref[...] = result
 
@@ -290,8 +308,9 @@
         for k in ORDER:
             node_copy(r, k).wait_send()
         for part in range(2):
-            for k in ORDER:
+            for k in (1, 3):
                 line_copy(r, part, k).wait_send()
+                half_copy(r, part, k).wait_send()
             for k in range(4):
                 side_copy(r, part, k).wait_send()
     for k in ORDER:
@@ -326,7 +345,7 @@
             pltpu.VMEM((EDGE, WIDTH), F32),
             pltpu.VMEM((EDGE, WIDTH), F32),
             dma((2,)), dma((2, 4)), dma((2, 4)), dma((2, 3)), dma((2, 3)), dma((3,)), dma((3,)),
-            dma((2,)), dma((2,)), dma((2, 2, 3)), dma((2, 2, 3)), dma((2, 2, 4)), dma((2, 2, 4)),
+            dma((2,)), dma((2,)), dma((2, 2, 3)), dma((2, 2, 3)), dma((2, 2, 3)), dma((2, 2, 3)), dma((2, 2, 4)), dma((2, 2, 4)),
         ],
         compiler_params=pltpu.CompilerParams(
             collective_id=0, has_side_effects=True, vmem_limit_bytes=56 * 1024 * 1024

time: 98.7 us -> 85 us (0.86)
  Pallas kernels: 93.8 us -> 80.4 us
    pallas_call x1, Pallas kernels: 93.8 us -> 80.4 us  [local(): pl.pallas_call(kernel, out_shape=(jax.ShapeDtypeStruct((NODE, WIDTH), BF1...]
where the time goes in v3:
time: 85 us; the launch traced here: 84.8 us
  Pallas kernels  80.4 us (95%)
  local copies, waits for them, and re-layouts  3.83 us (5%)
    pallas_call x1, Pallas kernels, local(): pl.pallas_call(kernel, out_shape=(jax.ShapeDtypeStruct((NODE, WIDTH), BF1...  80.4 us
    unnamed x2, local copies, waits for them, and re-layouts  3.83 us

profile of v3, /device:TPU:0, one launch (start us, length us, event | category | flops | bytes accessed | tf_op | source)
XLA Modules:
  0.0 84.8 jit_solution(205392815070458161)
XLA Ops:
  0.6 80.4 %shard_map.104 = (bf16[128,512]{1,0:T(8,128)(2,1)}, bf16[1024,512]{1,0:T(8,128)(2,1)}) custom-call(bf16[128,512]{1,0:T(8,128)(2,1)} %node_ref.1, bf16[1024,512]{1,0:T(8,128)(2,1)} %edge_ref.1, s32[8,128]{1,0:T(8,128)} %bitcast.12, s32[8,128]{1,0:T(8,128)} %bitcast.13, s32[16,128]{1,0:T(8,128)} %bitcast.11, bf16[2,3,2,16,512]{4,3,2,1,0:T(8,128)(2,1)} %bitcast.7, ...), custom_call_target="tpu_custom_call" | custom-call | tf_op jit(solution)/shard_map/pallas_call | solution.py:324
  81.0 1.6 %copy.13 = bf16[128,512]{1,0:T(8,128)(2,1)} copy(bf16[128,512]{1,0:T(8,128)(2,1)} %get-tuple-element.4) | data formatting | bytes 262144
  82.6 2.3 %copy.14 = bf16[1024,512]{1,0:T(8,128)(2,1)} copy(bf16[1024,512]{1,0:T(8,128)(2,1)} %get-tuple-element.5) | data formatting | bytes 2097152

commit v4 on v3

--- a/solution.py
+++ b/solution.py
@@ -42,7 +42,7 @@
     node_out_ref, edge_out_ref,
     weights, outgoing, table, node_mid, line_nodes, own_slots, line_slots,
     pick_local, pick_sender, pick_receiver, sum_receiver, pick_send, base, gathered,
-    load_sem, ex_send, ex_recv, node_send, node_recv, slot_send, slot_recv,
+    edges, ready, edge_sem, load_sem, ex_send, ex_recv, node_send, node_recv, slot_send, slot_recv,
     plane_send, plane_recv, line_send, line_recv, half_send, half_recv, side_send, side_recv,
 ):
     m = lax.axis_index("mesh")
@@ -65,11 +65,14 @@
     for k in ORDER:
         pl.semaphore_signal(barrier, inc=1, device_id=line(k), device_id_type=MESH)
 
+    pl.semaphore_signal(barrier, inc=1, device_id=sibling, device_id_type=MESH)
+
     def greet(j, carry):
-        pl.semaphore_signal(barrier, inc=1, device_id=peer(j)[1], device_id_type=MESH)
+        pl.semaphore_signal(barrier, inc=1, device_id=(m, lax.rem(c + j, 16)), device_id_type=MESH)
         return carry
 
-    lax.fori_loop(1, PLANE, greet, 0)
+    lax.fori_loop(1, 16, greet, 0)
+    pltpu.make_async_copy(edge_ref, edges, edge_sem.at[0]).start()
 
     columns = pl.ds(pl.multiple_of(x * 128, 128), 128)
     for r in range(2):
@@ -201,11 +204,13 @@
     make_pick(0)
     gather(0, 0)
 
-    pl.semaphore_wait(barrier, 34)
+    pl.semaphore_wait(barrier, 19)
+    pl.semaphore_signal(ready, inc=1, device_id=sibling, device_id_type=MESH)
     for k in ORDER:
         slot_copy(k).start()
         node_copy(0, k).start()
     start_plane(0)
+    pl.semaphore_wait(ready, 1)
     send(0, 0)
 
     eye = sub == lane
@@ -235,74 +240,97 @@
         gather(r, k)
         send(r, k)
 
-    start_plane(1)
+    def tiles(step):
+        def body(t, carry):
+            step(pl.ds(pl.multiple_of(t * TILE, TILE), TILE))
+            return carry
+        lax.fori_loop(0, EDGE // TILE, body, 0)
+
+    def picked(r, k, rows):
+        source = along(-k)
+        block = table[r, pl.ds(pl.multiple_of(source * PLANE_ROWS, PLANE_ROWS), PLANE_ROWS), :]
+        return mm(pick_sender[source, rows, :], block)
+
+    def arrive(r, k):
+        nodes = node_ref if r == 0 else node_mid
+        exchange_bytes(ex_recv.at[r, k]).wait()
+
+        def step(rows):
+            if k == 0:
+                gathered[rows, :] = mm(pick_local[rows, :], nodes[...]) + picked(r, k, rows)
+            else:
+                gathered[rows, :] += picked(r, k, rows)
+        tiles(step)
+
+    def before(r):
+        nodes = node_ref if r == 0 else node_mid
+        wait_side(r, 0)
+        recv_proj = mm(nodes[...], matrix(r, 2)).astype(BF16)
+
+        def step(rows):
+            base[rows, :] = mm(edges[rows, :], matrix(r, 0)) + mm(pick_receiver[rows, :], recv_proj)
+        tiles(step)
+
+    def after(r, k):
+        exchange_bytes(ex_recv.at[r, k]).wait()
+
+        def step(rows):
+            sender_rows = gathered[rows, :] + picked(r, k, rows)
+            preact = base[rows, :] + mm(sender_rows.astype(BF16), matrix(r, 1))
+            output = mm(silu(preact).astype(BF16), matrix(r, 3))
+            edges[rows, :] = (edges[rows, :].astype(F32) + norm_rows(output)).astype(BF16)
+        tiles(step)
+
+    def update(r):
+        nodes = node_ref if r == 0 else node_mid
+        wait_side(r, 1)
+        total = mm(sum_receiver[...], edges[...]).astype(BF16)
+        preact = mm(nodes[...], matrix(r, 4)) + mm(total, matrix(r, 5))
+        output = mm(silu(preact).astype(BF16), matrix(r, 6))
+        return (nodes[...].astype(F32) + norm_rows(output)).astype(BF16)
+
+    lax.fori_loop(0, EDGE // 128, edge_block, 0)
     start_line(0)
     relay(0, 1)
     relay(0, 3)
     pass_on(0, 0)
     relay(0, 2)
+    start_plane(1)
     pass_on(0, 1)
+    arrive(0, 0)
     finish_line(0, 0)
-    lax.fori_loop(0, EDGE // 128, edge_block, 0)
     finish_line(0, 1)
+    arrive(0, 1)
+    pltpu.make_async_copy(edge_ref, edges, edge_sem.at[0]).wait()
+    before(0)
+    arrive(0, 3)
+    after(0, 2)
+    node_mid[...] = update(0)
+
+    for k in ORDER:
+        node_copy(1, k).start()
+    for k in range(4):
+        exchange_bytes(ex_send.at[0, k]).wait()
+    gather(1, 0)
+    send(1, 0)
     start_line(1)
-
-    for r in range(2):
-        nodes = node_ref if r == 0 else node_mid
-        edges = edge_ref if r == 0 else edge_out_ref
-        wait_side(r, 0)
-        recv_proj = mm(nodes[...], matrix(r, 2)).astype(BF16)
-
-        def before(t, carry):
-            rows = pl.ds(pl.multiple_of(t * TILE, TILE), TILE)
-            base[rows, :] = mm(edges[rows, :], matrix(r, 0)) + mm(pick_receiver[rows, :], recv_proj)
-            gathered[rows, :] = mm(pick_local[rows, :], nodes[...])
-            return carry
-
-        lax.fori_loop(0, EDGE // TILE, before, 0)
-        for k in (0,) + ORDER:
-            exchange_bytes(ex_recv.at[r, k]).wait()
-            source = along(-k)
-
-            def arrive(t, carry):
-                rows = pl.ds(pl.multiple_of(t * TILE, TILE), TILE)
-                block = table[r, pl.ds(pl.multiple_of(source * PLANE_ROWS, PLANE_ROWS), PLANE_ROWS), :]
-                gathered[rows, :] += mm(pick_sender[source, rows, :], block)
-                return carry
-
-            lax.fori_loop(0, EDGE // TILE, arrive, 0)
-        if r == 0:
-            pass_on(1, 0)
-
-        def after(t, carry):
-            rows = pl.ds(pl.multiple_of(t * TILE, TILE), TILE)
-            preact = base[rows, :] + mm(gathered[rows, :].astype(BF16), matrix(r, 1))
-            output = mm(silu(preact).astype(BF16), matrix(r, 3))
-            edge_out_ref[rows, :] = (edges[rows, :].astype(F32) + norm_rows(output)).astype(BF16)
-            return carry
-
-        lax.fori_loop(0, EDGE // TILE, after, 0)
-        wait_side(r, 1)
-        total = mm(sum_receiver[...], edge_out_ref[...]).astype(BF16)
-        preact = mm(nodes[...], matrix(r, 4)) + mm(total, matrix(r, 5))
-        output = mm(silu(preact).astype(BF16), matrix(r, 6))
-        result = (nodes[...].astype(F32) + norm_rows(output)).astype(BF16)
-        for k in range(4):
-            exchange_bytes(ex_send.at[r, k]).wait()
-        if r == 0:
-            node_mid[...] = result
-            for k in ORDER:
-                node_copy(1, k).start()
-            gather(1, 0)
-            send(1, 0)
-            for k in ORDER:
-                relay(1, k)
-            finish_line(1, 0)
-            pass_on(1, 1)
-            finish_line(1, 1)
-        else:
-            node_out_ref[...] = result
-
+    for k in ORDER:
+        relay(1, k)
+    pass_on(1, 0)
+    arrive(1, 0)
+    pass_on(1, 1)
+    arrive(1, 1)
+    finish_line(1, 0)
+    arrive(1, 3)
+    finish_line(1, 1)
+    before(1)
+    after(1, 2)
+    pltpu.make_async_copy(edges, edge_out_ref, edge_sem.at[1]).start()
+    node_out_ref[...] = update(1)
+
+    for k in range(4):
+        exchange_bytes(ex_send.at[1, k]).wait()
+    pltpu.make_async_copy(edges, edge_out_ref, edge_sem.at[1]).wait()
     for r in range(2):
         plane_bytes(r, plane_send).wait()
         for k in ORDER:
@@ -327,8 +355,8 @@
             jax.ShapeDtypeStruct((NODE, WIDTH), BF16),
             jax.ShapeDtypeStruct((EDGE, WIDTH), BF16),
         ),
-        in_specs=[vmem] * 5 + [anywhere] * 4,
-        out_specs=(vmem, vmem),
+        in_specs=[vmem, anywhere] + [vmem] * 3 + [anywhere] * 4,
+        out_specs=(vmem, anywhere),
         scratch_shapes=[
             pltpu.VMEM((2, 4, 16, 2, 7, 16, 128), BF16),
             pltpu.VMEM((4, PLANE_ROWS, WIDTH), BF16),
@@ -344,7 +372,9 @@
             pltpu.VMEM((4, PLANE_ROWS, NODE), BF16),
             pltpu.VMEM((EDGE, WIDTH), F32),
             pltpu.VMEM((EDGE, WIDTH), F32),
-            dma((2,)), dma((2, 4)), dma((2, 4)), dma((2, 3)), dma((2, 3)), dma((3,)), dma((3,)),
+            pltpu.VMEM((EDGE, WIDTH), BF16),
+            pltpu.SemaphoreType.REGULAR,
+            dma((2,)), dma((2,)), dma((2, 4)), dma((2, 4)), dma((2, 3)), dma((2, 3)), dma((3,)), dma((3,)),
             dma((2,)), dma((2,)), dma((2, 2, 3)), dma((2, 2, 3)), dma((2, 2, 3)), dma((2, 2, 3)), dma((2, 2, 4)), dma((2, 2, 4)),
         ],
         compiler_params=pltpu.CompilerParams(

time: 85 us -> 79.3 us (0.933)
  Pallas kernels: 80.4 us -> 74.5 us
    pallas_call x1, Pallas kernels: 80.4 us -> 74.5 us  [local(): pl.pallas_call(kernel, out_shape=(jax.ShapeDtypeStruct((NODE, WIDTH), BF1...]
where the time goes in v4:
time: 79.3 us; the launch traced here: 78.9 us
  Pallas kernels  74.5 us (94%)
  local copies, waits for them, and re-layouts  3.83 us (5%)
    pallas_call x1, Pallas kernels, local(): pl.pallas_call(kernel, out_shape=(jax.ShapeDtypeStruct((NODE, WIDTH), BF1...  74.5 us
    unnamed x2, local copies, waits for them, and re-layouts  3.83 us

profile of v4, /device:TPU:0, one launch (start us, length us, event | category | flops | bytes accessed | tf_op | source)
XLA Modules:
  0.0 78.9 jit_solution(7181628320641532130)
XLA Ops:
  0.6 74.5 %shard_map.104 = (bf16[128,512]{1,0:T(8,128)(2,1)}, bf16[1024,512]{1,0:T(8,128)(2,1)}) custom-call(bf16[128,512]{1,0:T(8,128)(2,1)} %node_ref.1, bf16[1024,512]{1,0:T(8,128)(2,1)} %edge_ref.1, s32[8,128]{1,0:T(8,128)} %bitcast.12, s32[8,128]{1,0:T(8,128)} %bitcast.13, s32[16,128]{1,0:T(8,128)} %bitcast.11, bf16[2,3,2,16,512]{4,3,2,1,0:T(8,128)(2,1)} %bitcast.7, ...), custom_call_target="tpu_custom_call" | custom-call | tf_op jit(solution)/shard_map/pallas_call | solution.py:352
  75.1 1.6 %copy.13 = bf16[128,512]{1,0:T(8,128)(2,1)} copy(bf16[128,512]{1,0:T(8,128)(2,1)} %get-tuple-element.4) | data formatting | bytes 262144
  76.7 2.3 %copy.14 = bf16[1024,512]{1,0:T(8,128)(2,1)} copy(bf16[1024,512]{1,0:T(8,128)(2,1)} %get-tuple-element.5) | data formatting | bytes 2097152

commit v5 on v4

--- a/solution.py
+++ b/solution.py
@@ -34,15 +34,16 @@
 
 
 def silu(v):
-    return v / (1.0 + jnp.exp(-v))
+    half = 0.5 * v
+    return half + half * jnp.tanh(half)
 
 
 def kernel(
-    node_ref, edge_ref, sender_ref, receiver_ref, slots_ref, ein, eout, nin, nout,
+    node_in, edge_ref, sender_in, receiver_in, slots_in, ein, eout, nin, nout,
     node_out_ref, edge_out_ref,
     weights, outgoing, table, node_mid, line_nodes, own_slots, line_slots,
     pick_local, pick_sender, pick_receiver, sum_receiver, pick_send, base, gathered,
-    edges, ready, edge_sem, load_sem, ex_send, ex_recv, node_send, node_recv, slot_send, slot_recv,
+    node_ref, sender_ref, receiver_ref, slots_ref, edges, projected, ready, small_sem, edge_sem, load_sem, ex_send, ex_recv, node_send, node_recv, slot_send, slot_recv,
     plane_send, plane_recv, line_send, line_recv, half_send, half_recv, side_send, side_recv,
 ):
     m = lax.axis_index("mesh")
@@ -57,10 +58,6 @@
     def line(k):
         return (along(k) * 2 + core, c)
 
-    def peer(j):
-        q = lax.rem(own + j, PLANE)
-        return q, (x * 2 + q // 16, lax.rem(q, 16))
-
     barrier = pltpu.get_barrier_semaphore()
     for k in ORDER:
         pl.semaphore_signal(barrier, inc=1, device_id=line(k), device_id_type=MESH)
@@ -72,6 +69,14 @@
         return carry
 
     lax.fori_loop(1, 16, greet, 0)
+    smalls = [
+        pltpu.make_async_copy(src, dst, small_sem.at[i])
+        for i, (src, dst) in enumerate(
+            ((slots_in, slots_ref), (node_in, node_ref), (sender_in, sender_ref), (receiver_in, receiver_ref))
+        )
+    ]
+    for small in smalls:
+        small.start()
     pltpu.make_async_copy(edge_ref, edges, edge_sem.at[0]).start()
 
     columns = pl.ds(pl.multiple_of(x * 128, 128), 128)
@@ -183,21 +188,28 @@
         return table.at[r, pl.ds(pl.multiple_of(at, SLOT), SLOT)]
 
     def send(r, k):
-        def step(j, carry):
-            q, device = peer(j)
-            src = outgoing.at[k, pl.ds(pl.multiple_of(q * SLOT, SLOT), SLOT)]
-            remote(src, landing(r, k), ex_send.at[r, k], ex_recv.at[r, k], device).start()
-            return carry
-        lax.fori_loop(1, PLANE, step, 0)
+        for side in range(2):
+            def step(j, carry):
+                chan = lax.rem(c + j, 16)
+                to_core = lax.rem(core + side, 2)
+                q = to_core * 16 + chan
+                src = outgoing.at[k, pl.ds(pl.multiple_of(q * SLOT, SLOT), SLOT)]
+                remote(
+                    src, landing(r, k), ex_send.at[r, k, side], ex_recv.at[r, k, side], (x * 2 + to_core, chan)
+                ).start()
+                return carry
+            lax.fori_loop(1 - side, 16, step, 0)
         if k:
             landing(r, k)[...] = outgoing[k, pl.ds(pl.multiple_of(own * SLOT, SLOT), SLOT), :]
         else:
             landing(r, k)[...] = jnp.zeros((SLOT, WIDTH), BF16)
 
-    def exchange_bytes(sem):
-        ref = outgoing.at[0, pl.ds(0, (PLANE - 1) * SLOT)]
-        return pltpu.make_async_copy(ref, ref, sem)
-
+    def wait_exchange(sem, r, k, side):
+        ref = outgoing.at[0, pl.ds(0, (15 + side) * SLOT)]
+        pltpu.make_async_copy(ref, ref, sem.at[r, k, side]).wait()
+
+    for small in smalls:
+        small.wait()
     slots = jnp.concatenate([slots_ref[...].astype(F32), jnp.zeros((128 - SLOT, 128), F32)], axis=0)
     own_slots[...] = jnp.transpose(slots).astype(BF16)
     line_slots[0] = own_slots[pl.ds(pl.multiple_of(x * PLANE, PLANE), PLANE), :]
@@ -241,10 +253,8 @@
         send(r, k)
 
     def tiles(step):
-        def body(t, carry):
-            step(pl.ds(pl.multiple_of(t * TILE, TILE), TILE))
-            return carry
-        lax.fori_loop(0, EDGE // TILE, body, 0)
+        for t in range(EDGE // TILE):
+            step(slice(t * TILE, (t + 1) * TILE))
 
     def picked(r, k, rows):
         source = along(-k)
@@ -253,7 +263,8 @@
 
     def arrive(r, k):
         nodes = node_ref if r == 0 else node_mid
-        exchange_bytes(ex_recv.at[r, k]).wait()
+        for side in range(2):
+            wait_exchange(ex_recv, r, k, side)
 
         def step(rows):
             if k == 0:
@@ -268,15 +279,21 @@
         recv_proj = mm(nodes[...], matrix(r, 2)).astype(BF16)
 
         def step(rows):
-            base[rows, :] = mm(edges[rows, :], matrix(r, 0)) + mm(pick_receiver[rows, :], recv_proj)
+            total = mm(edges[rows, :], matrix(r, 0)) + mm(pick_receiver[rows, :], recv_proj)
+            base[rows, :] = total + mm(gathered[rows, :].astype(BF16), matrix(r, 1))
         tiles(step)
 
     def after(r, k):
-        exchange_bytes(ex_recv.at[r, k]).wait()
+        source = along(-k)
+        half = PLANE_ROWS // 2
+        for side in range(2):
+            wait_exchange(ex_recv, r, k, side)
+            at = lax.rem(core + side, 2) * half
+            block = table[r, pl.ds(pl.multiple_of(source * PLANE_ROWS + at, half), half), :]
+            projected[pl.ds(pl.multiple_of(at, half), half), :] = mm(block, matrix(r, 1)).astype(BF16)
 
         def step(rows):
-            sender_rows = gathered[rows, :] + picked(r, k, rows)
-            preact = base[rows, :] + mm(sender_rows.astype(BF16), matrix(r, 1))
+            preact = base[rows, :] + mm(pick_sender[source, rows, :], projected[...])
             output = mm(silu(preact).astype(BF16), matrix(r, 3))
             edges[rows, :] = (edges[rows, :].astype(F32) + norm_rows(output)).astype(BF16)
         tiles(step)
@@ -301,16 +318,17 @@
     finish_line(0, 0)
     finish_line(0, 1)
     arrive(0, 1)
+    arrive(0, 3)
     pltpu.make_async_copy(edge_ref, edges, edge_sem.at[0]).wait()
     before(0)
-    arrive(0, 3)
     after(0, 2)
     node_mid[...] = update(0)
 
     for k in ORDER:
         node_copy(1, k).start()
     for k in range(4):
-        exchange_bytes(ex_send.at[0, k]).wait()
+        for side in range(2):
+            wait_exchange(ex_send, 0, k, side)
     gather(1, 0)
     send(1, 0)
     start_line(1)
@@ -329,7 +347,8 @@
     node_out_ref[...] = update(1)
 
     for k in range(4):
-        exchange_bytes(ex_send.at[1, k]).wait()
+        for side in range(2):
+            wait_exchange(ex_send, 1, k, side)
     pltpu.make_async_copy(edges, edge_out_ref, edge_sem.at[1]).wait()
     for r in range(2):
         plane_bytes(r, plane_send).wait()
@@ -345,17 +364,33 @@
         slot_copy(k).wait_send()
 
 
+def hand_out(node_ref, edge_ref, node_out_ref, edge_out_ref, node_buf, edge_buf, sems):
+    pieces = [(node_ref, node_buf, node_out_ref)]
+    for i in range(4):
+        rows = pl.ds(i * (EDGE // 4), EDGE // 4)
+        pieces.append((edge_ref.at[rows], edge_buf.at[rows], edge_out_ref.at[rows]))
+    loads = [pltpu.make_async_copy(src, buf, sems.at[0, i]) for i, (src, buf, _) in enumerate(pieces)]
+    stores = [pltpu.make_async_copy(buf, dst, sems.at[1, i]) for i, (_, buf, dst) in enumerate(pieces)]
+    for load in loads:
+        load.start()
+    for load, store in zip(loads, stores):
+        load.wait()
+        store.start()
+    for store in stores:
+        store.wait()
+
+
 def local(node_latents, edge_latents, sender_slot, receiver_node, send_rows, edge_in, edge_out, node_in, node_out):
     vmem = pl.BlockSpec(memory_space=pltpu.VMEM)
     anywhere = pl.BlockSpec(memory_space=pl.ANY)
     dma = pltpu.SemaphoreType.DMA
-    return pl.pallas_call(
+    node_state, edge_state = pl.pallas_call(
         kernel,
         out_shape=(
             jax.ShapeDtypeStruct((NODE, WIDTH), BF16),
             jax.ShapeDtypeStruct((EDGE, WIDTH), BF16),
         ),
-        in_specs=[vmem, anywhere] + [vmem] * 3 + [anywhere] * 4,
+        in_specs=[anywhere] * 9,
         out_specs=(vmem, anywhere),
         scratch_shapes=[
             pltpu.VMEM((2, 4, 16, 2, 7, 16, 128), BF16),
@@ -372,9 +407,15 @@
             pltpu.VMEM((4, PLANE_ROWS, NODE), BF16),
             pltpu.VMEM((EDGE, WIDTH), F32),
             pltpu.VMEM((EDGE, WIDTH), F32),
+            pltpu.VMEM((NODE, WIDTH), BF16),
+            pltpu.VMEM((8, 128), jnp.int32),
+            pltpu.VMEM((8, 128), jnp.int32),
+            pltpu.VMEM((SLOT, 128), jnp.int32),
             pltpu.VMEM((EDGE, WIDTH), BF16),
+            pltpu.VMEM((PLANE_ROWS, WIDTH), BF16),
             pltpu.SemaphoreType.REGULAR,
-            dma((2,)), dma((2,)), dma((2, 4)), dma((2, 4)), dma((2, 3)), dma((2, 3)), dma((3,)), dma((3,)),
+            dma((4,)),
+            dma((2,)), dma((2,)), dma((2, 4, 2)), dma((2, 4, 2)), dma((2, 3)), dma((2, 3)), dma((3,)), dma((3,)),
             dma((2,)), dma((2,)), dma((2, 2, 3)), dma((2, 2, 3)), dma((2, 2, 3)), dma((2, 2, 3)), dma((2, 2, 4)), dma((2, 2, 4)),
         ],
         compiler_params=pltpu.CompilerParams(
@@ -391,6 +432,16 @@
         node_in.reshape(2, 2, 2, 16, WIDTH),
         node_out.reshape(2, 2, 16, WIDTH),
     )
+    return pl.pallas_call(
+        hand_out,
+        out_shape=(
+            jax.ShapeDtypeStruct((NODE, WIDTH), BF16),
+            jax.ShapeDtypeStruct((EDGE, WIDTH), BF16),
+        ),
+        in_specs=[anywhere] * 2,
+        out_specs=(anywhere, anywhere),
+        scratch_shapes=[pltpu.VMEM((NODE, WIDTH), BF16), pltpu.VMEM((EDGE, WIDTH), BF16), dma((2, 5))],
+    )(node_state, edge_state)
 
 
 def solution(mesh):

time: 79.3 us -> 74.4 us (0.938)
  local copies, waits for them, and re-layouts: 3.83 us -> 0 us
  Pallas kernels: 74.5 us -> 73.6 us
    unnamed x2 -> x0, local copies, waits for them, and re-layouts: 3.83 us -> none
    pallas_call x1, Pallas kernels: 74.5 us -> 71.5 us  [local(): pl.pallas_call(kernel, out_shape=(jax.ShapeDtypeStruct((NODE, WIDTH), BF1...]
    pallas_call x0 -> x1, Pallas kernels: none -> 2.07 us  [local(): pl.pallas_call(hand_out, out_shape=(jax.ShapeDtypeStruct((NODE, WIDTH), B...]
where the time goes in v5:
time: 74.4 us; the launch traced here: 74.3 us
  Pallas kernels  73.6 us (99%)
    pallas_call x1, Pallas kernels, local(): pl.pallas_call(kernel, out_shape=(jax.ShapeDtypeStruct((NODE, WIDTH), BF1...  71.5 us
    pallas_call x1, Pallas kernels, local(): pl.pallas_call(hand_out, out_shape=(jax.ShapeDtypeStruct((NODE, WIDTH), B...  2.07 us

profile of v5, /device:TPU:0, one launch (start us, length us, event | category | flops | bytes accessed | tf_op | source)
XLA Modules:
  0.0 74.3 jit_solution(14642040905275822299)
XLA Ops:
  0.6 71.5 %shard_map.104 = (bf16[128,512]{1,0:T(8,128)(2,1)}, bf16[1024,512]{1,0:T(8,128)(2,1)}) custom-call(bf16[128,512]{1,0:T(8,128)(2,1)} %node_in.1, bf16[1024,512]{1,0:T(8,128)(2,1)} %edge_ref.1, s32[8,128]{1,0:T(8,128)} %bitcast.12, s32[8,128]{1,0:T(8,128)} %bitcast.13, s32[16,128]{1,0:T(8,128)} %bitcast.11, bf16[2,3,2,16,512]{4,3,2,1,0:T(8,128)(2,1)} %bitcast.7, ...), custom_call_target="tpu_custom_call" | custom-call | tf_op jit(solution)/shard_map/pallas_call | solution.py:387
  72.2 2.1 %shard_map.105 = (bf16[128,512]{1,0:T(8,128)(2,1)}, bf16[1024,512]{1,0:T(8,128)(2,1)}) custom-call(bf16[128,512]{1,0:T(8,128)(2,1)} %get-tuple-element.4.node_ref, bf16[1024,512]{1,0:T(8,128)(2,1)} %get-tuple-element.5.edge_ref), custom_call_target="tpu_custom_call" | custom-call | tf_op jit(solution)/shard_map/pallas_call | solution.py:435

commit v6 on v5

--- a/solution.py
+++ b/solution.py
@@ -245,9 +245,6 @@
         return carry
 
     def relay(r, k):
-        if r == 0:
-            slot_copy(k).wait_recv()
-            make_pick(k)
         node_copy(r, k).wait_recv()
         gather(r, k)
         send(r, k)
@@ -307,6 +304,9 @@
         return (nodes[...].astype(F32) + norm_rows(output)).astype(BF16)
 
     lax.fori_loop(0, EDGE // 128, edge_block, 0)
+    for k in ORDER:
+        slot_copy(k).wait_recv()
+        make_pick(k)
     start_line(0)
     relay(0, 1)
     relay(0, 3)
@@ -316,11 +316,11 @@
     pass_on(0, 1)
     arrive(0, 0)
     finish_line(0, 0)
-    finish_line(0, 1)
     arrive(0, 1)
     arrive(0, 3)
     pltpu.make_async_copy(edge_ref, edges, edge_sem.at[0]).wait()
     before(0)
+    finish_line(0, 1)
     after(0, 2)
     node_mid[...] = update(0)
 
@@ -340,8 +340,8 @@
     arrive(1, 1)
     finish_line(1, 0)
     arrive(1, 3)
+    before(1)
     finish_line(1, 1)
-    before(1)
     after(1, 2)
     pltpu.make_async_copy(edges, edge_out_ref, edge_sem.at[1]).start()
     node_out_ref[...] = update(1)

time: 74.4 us -> 74.4 us (level); the launches traced: 74.3 us -> 73.4 us
  Pallas kernels: 73.6 us -> 72.8 us
    pallas_call x1, Pallas kernels: 71.5 us -> 70.7 us  [local(): pl.pallas_call(kernel, out_shape=(jax.ShapeDtypeStruct((NODE, WIDTH), BF1...]
where the time goes in v6:
time: 74.4 us; the launch traced here: 73.4 us
  Pallas kernels  72.8 us (98%)
    pallas_call x1, Pallas kernels, local(): pl.pallas_call(kernel, out_shape=(jax.ShapeDtypeStruct((NODE, WIDTH), BF1...  70.7 us
    pallas_call x1, Pallas kernels, local(): pl.pallas_call(hand_out, out_shape=(jax.ShapeDtypeStruct((NODE, WIDTH), B...  2.07 us

profile of v6, /device:TPU:0, one launch (start us, length us, event | category | flops | bytes accessed | tf_op | source)
XLA Modules:
  0.0 73.4 jit_solution(409826388647924505)
XLA Ops:
  0.6 70.7 %shard_map.104 = (bf16[128,512]{1,0:T(8,128)(2,1)}, bf16[1024,512]{1,0:T(8,128)(2,1)}) custom-call(bf16[128,512]{1,0:T(8,128)(2,1)} %node_in.1, bf16[1024,512]{1,0:T(8,128)(2,1)} %edge_ref.1, s32[8,128]{1,0:T(8,128)} %bitcast.12, s32[8,128]{1,0:T(8,128)} %bitcast.13, s32[16,128]{1,0:T(8,128)} %bitcast.11, bf16[2,3,2,16,512]{4,3,2,1,0:T(8,128)(2,1)} %bitcast.7, ...), custom_call_target="tpu_custom_call" | custom-call | tf_op jit(solution)/shard_map/pallas_call | solution.py:387
  71.4 2.1 %shard_map.105 = (bf16[128,512]{1,0:T(8,128)(2,1)}, bf16[1024,512]{1,0:T(8,128)(2,1)}) custom-call(bf16[128,512]{1,0:T(8,128)(2,1)} %get-tuple-element.4.node_ref, bf16[1024,512]{1,0:T(8,128)(2,1)} %get-tuple-element.5.edge_ref), custom_call_target="tpu_custom_call" | custom-call | tf_op jit(solution)/shard_map/pallas_call | solution.py:435

commit v7 on v5

--- a/solution.py
+++ b/solution.py
@@ -59,16 +59,14 @@
         return (along(k) * 2 + core, c)
 
     barrier = pltpu.get_barrier_semaphore()
-    for k in ORDER:
-        pl.semaphore_signal(barrier, inc=1, device_id=line(k), device_id_type=MESH)
-
-    pl.semaphore_signal(barrier, inc=1, device_id=sibling, device_id_type=MESH)
-
     def greet(j, carry):
         pl.semaphore_signal(barrier, inc=1, device_id=(m, lax.rem(c + j, 16)), device_id_type=MESH)
         return carry
 
     lax.fori_loop(1, 16, greet, 0)
+    for k in (2, 1, 3):
+        pl.semaphore_signal(barrier, inc=1, device_id=line(k), device_id_type=MESH)
+    pl.semaphore_signal(barrier, inc=1, device_id=sibling, device_id_type=MESH)
     smalls = [
         pltpu.make_async_copy(src, dst, small_sem.at[i])
         for i, (src, dst) in enumerate(
@@ -366,8 +364,8 @@
 
 def hand_out(node_ref, edge_ref, node_out_ref, edge_out_ref, node_buf, edge_buf, sems):
     pieces = [(node_ref, node_buf, node_out_ref)]
-    for i in range(4):
-        rows = pl.ds(i * (EDGE // 4), EDGE // 4)
+    for i in range(8):
+        rows = pl.ds(i * (EDGE // 8), EDGE // 8)
         pieces.append((edge_ref.at[rows], edge_buf.at[rows], edge_out_ref.at[rows]))
     loads = [pltpu.make_async_copy(src, buf, sems.at[0, i]) for i, (src, buf, _) in enumerate(pieces)]
     stores = [pltpu.make_async_copy(buf, dst, sems.at[1, i]) for i, (_, buf, dst) in enumerate(pieces)]
@@ -440,7 +438,7 @@
         ),
         in_specs=[anywhere] * 2,
         out_specs=(anywhere, anywhere),
-        scratch_shapes=[pltpu.VMEM((NODE, WIDTH), BF16), pltpu.VMEM((EDGE, WIDTH), BF16), dma((2, 5))],
+        scratch_shapes=[pltpu.VMEM((NODE, WIDTH), BF16), pltpu.VMEM((EDGE, WIDTH), BF16), dma((2, 9))],
     )(node_state, edge_state)
 
 

time: 74.4 us -> 74.5 us (level)
  no operation moved by 1% of the time
where the time goes in v7:
time: 74.5 us; the launch traced here: 73.8 us
  Pallas kernels  73.1 us (98%)
    pallas_call x1, Pallas kernels, local(): pl.pallas_call(kernel, out_shape=(jax.ShapeDtypeStruct((NODE, WIDTH), BF1...  71 us
    pallas_call x1, Pallas kernels, local(): pl.pallas_call(hand_out, out_shape=(jax.ShapeDtypeStruct((NODE, WIDTH), B...  2.15 us

profile of v7, /device:TPU:0, one launch (start us, length us, event | category | flops | bytes accessed | tf_op | source)
XLA Modules:
  0.0 73.8 jit_solution(12816311526133421423)
XLA Ops:
  0.6 71.0 %shard_map.104 = (bf16[128,512]{1,0:T(8,128)(2,1)}, bf16[1024,512]{1,0:T(8,128)(2,1)}) custom-call(bf16[128,512]{1,0:T(8,128)(2,1)} %node_in.1, bf16[1024,512]{1,0:T(8,128)(2,1)} %edge_ref.1, s32[8,128]{1,0:T(8,128)} %bitcast.12, s32[8,128]{1,0:T(8,128)} %bitcast.13, s32[16,128]{1,0:T(8,128)} %bitcast.11, bf16[2,3,2,16,512]{4,3,2,1,0:T(8,128)(2,1)} %bitcast.7, ...), custom_call_target="tpu_custom_call" | custom-call | tf_op jit(solution)/shard_map/pallas_call | solution.py:385
  71.6 2.1 %shard_map.105 = (bf16[128,512]{1,0:T(8,128)(2,1)}, bf16[1024,512]{1,0:T(8,128)(2,1)}) custom-call(bf16[128,512]{1,0:T(8,128)(2,1)} %get-tuple-element.4.node_ref, bf16[1024,512]{1,0:T(8,128)(2,1)} %get-tuple-element.5.edge_ref), custom_call_target="tpu_custom_call" | custom-call | tf_op jit(solution)/shard_map/pallas_call | solution.py:433
